TPU v7x, 128 devices: a whole 4x4x4 slice. The times are simulated.
128 devices in a mesh: tm: 8 (over y, core), seq: 16 (over x, z).
Axes of the slice: x: 4, y: 4, z: 4, core: 2. Of those that a mesh axis runs over, the one named last changes fastest.
Arguments:
- queries: bfloat16 [8, 4096, 2048], P('tm', 'seq'), may hold values from -6 to 6
- keys: bfloat16 [8, 4480, 2048], P('tm', 'seq'), may hold values from -6 to 6
- values: bfloat16 [8, 4480, 2048], P('tm', 'seq'), may hold values from -6 to 6
- hidden: bfloat16 [8, 4096, 2432], P('tm', 'seq'), may hold values from -0.119628906 to 0.119628906
- w_proj: bfloat16 [2048, 2432], replicated, may hold values from -0.125 to 0.125
- w_final: bfloat16 [2432, 64], replicated, may hold values from -0.125 to 0.125
- gate_base: float32 [2432], replicated, may hold values from -6 to 6
- gate_slope: float32 [2432], replicated, may hold values from -6 to 6
- start_latent: float32 [4096, 64], P('seq'), may hold values from -6 to 6
- window_steps: int32 [9], replicated, may hold values from 0 to 16, as said below
Outputs:
- velocity: float32 [8, 4096, 64], P('tm', 'seq')
- latents: float32 [8, 4096, 64], P('tm', 'seq')
Inputs may be any that keep to these rules, and one draw needn't show every extreme that they name: window_steps[0] is 0, the last entry is 16, and each entry exceeds the one before by 1 to 3.
All inputs are finite; a program needn't handle non-finite values.
Results may differ from a plain program's by a relative error of at most 0.0059.
Values may be sent and summed in bfloat16 or wider, within the bound.
No kernel may reach another device: no remote copies, remote signals or barrier semaphores. Data moves between devices by JAX's collectives and lax.ppermute only.
A program may use at most 192 MiB of HBM per device.

v0:
```python
import functools

import jax
import jax.numpy as jnp
from jax import lax
from jax.experimental import pallas as pl
from jax.experimental.pallas import tpu as pltpu
from jax.sharding import PartitionSpec as P

HEADS = 32
HEAD_DIM = 64
HD = 2048
D = 2432
LAT = 64
PAIR = 128
RING = 4
SLOTS = 8
BOTH = ("tm", "seq")
NT = (((1,), (1,)), ((), ()))
SCALE = 0.125 * 1.4426950408889634
KEY_CUTS = ((0, 96), (96, 280))
QROWS = 256
KROWS = 280
TILE = 512
BLOCK_Q = 2048
STEP_Q = 1024
VROWS = 128
MIB = 2**20


def swap_pairs(first, mask):
    pairs = []
    for slot in range(8):
        for place in range(16):
            x, z = divmod(place, RING)
            if (slot % 2 == 0) == first:
                x2, z2 = x ^ mask, z
            else:
                x2, z2 = x, z ^ mask
            pairs.append((slot * 16 + place, slot * 16 + x2 * RING + z2))
    return pairs


def send(value, first, mask):
    return lax.ppermute(value, BOTH, swap_pairs(first, mask))


def head_norm(block):
    wide = block.astype(jnp.float32)
    square = wide * wide
    high = square.astype(jnp.bfloat16)
    low = (square - high.astype(jnp.float32)).astype(jnp.bfloat16)
    row = lax.broadcasted_iota(jnp.int32, (PAIR, PAIR), 0)
    col = lax.broadcasted_iota(jnp.int32, (PAIR, PAIR), 1)
    same = ((row < HEAD_DIM) == (col < HEAD_DIM)).astype(jnp.bfloat16)
    total = jnp.dot(high, same, preferred_element_type=jnp.float32)
    total = total + jnp.dot(low, same, preferred_element_type=jnp.float32)
    return (wide * lax.rsqrt(total * (1.0 / HEAD_DIM) + 1e-06)).astype(jnp.bfloat16)


def padded(rows):
    return -(-rows // 16) * 16


def layout():
    at, places = QROWS, []
    for k0, k1 in KEY_CUTS:
        places.append((at, at + padded(k1 - k0)))
        at += 2 * padded(k1 - k0)
    return places, at


def pack_kernel(shifts, q_hbm, k_hbm, v_hbm, *refs):
    seat, odd = lax.axis_index("seq"), lax.rem(lax.axis_index("tm"), 2)
    x, z = seat // RING, lax.rem(seat, RING)
    first, second = x + odd * (z - x), z + odd * (x - z)
    outs, (q_buf, k_buf, v_buf, sems) = refs[: len(shifts)], refs[len(shifts) :]
    places, _ = layout()
    copies = []
    for i, d in enumerate(shifts):
        group = first ^ d
        lanes = pl.ds(pl.multiple_of(group * (RING * PAIR), RING * PAIR), RING * PAIR)
        copies.append(
            [
                pltpu.make_async_copy(source.at[:, lanes], target.at[i], sems.at[i, n])
                for n, (source, target) in enumerate(((q_hbm, q_buf), (k_hbm, k_buf), (v_hbm, v_buf)))
            ]
        )
        for copy in copies[i]:
            copy.start()
    for i in range(len(shifts)):
        for copy in copies[i]:
            copy.wait()
        out = outs[i]
        for e in range(RING):
            pair = second ^ e
            lanes = pl.ds(pl.multiple_of(pair * PAIR, PAIR), PAIR)
            out[e, 0:QROWS] = head_norm(q_buf[i, :, lanes])
            keys = head_norm(k_buf[i, :, lanes])
            for (k0, k1), (kp, vp) in zip(KEY_CUTS, places):
                out[e, kp : kp + k1 - k0] = keys[k0:k1]
                out[e, vp : vp + k1 - k0] = v_buf[i, k0:k1, lanes]
                gap = padded(k1 - k0) - (k1 - k0)
                if gap:
                    out[e, vp - gap : vp] = jnp.zeros((gap, PAIR), jnp.bfloat16)
                    out[e, vp + k1 - k0 : vp + k1 - k0 + gap] = jnp.zeros((gap, PAIR), jnp.bfloat16)


def pack(queries, keys, values, shifts):
    _, rows = layout()
    vmem = pl.BlockSpec(memory_space=pltpu.VMEM)
    wide = RING * PAIR
    count = len(shifts)
    return pl.pallas_call(
        functools.partial(pack_kernel, shifts),
        in_specs=[pl.BlockSpec(memory_space=pltpu.HBM)] * 3,
        out_specs=[vmem] * count,
        out_shape=[jax.ShapeDtypeStruct((RING, rows, PAIR), jnp.bfloat16)] * count,
        scratch_shapes=[
            pltpu.VMEM((count, QROWS, wide), jnp.bfloat16),
            pltpu.VMEM((count, KROWS, wide), jnp.bfloat16),
            pltpu.VMEM((count, KROWS, wide), jnp.bfloat16),
            pltpu.SemaphoreType.DMA((count, 3)),
        ],
        compiler_params=pltpu.CompilerParams(vmem_limit_bytes=59 * MIB),
        cost_estimate=pl.CostEstimate(
            flops=count * rows * HD * PAIR, bytes_accessed=count * rows * HD, transcendentals=0
        ),
        name="pack",
    )(queries, keys, values)


def first_hop(queries, keys, values):
    up, down, across, own = pack(queries, keys, values, (1, 3, 2, 0))
    return [own, send(up, True, 1), send(across, True, 2), send(down, True, 3)]


def second_hop(landed, start, stop):
    staged = [jnp.stack([part[e, start:stop] for part in landed]) for e in range(RING)]
    return [staged[0]] + [send(staged[e], False, e) for e in range(1, RING)]


def cuts_of(total, step):
    return [(start, min(step, total - start)) for start in range(0, total, step)]


def attend_kernel(count, q_from, key_from, groups, before, last, place_ref, *refs):
    parts, refs = refs[:count], refs[count:]
    if before:
        acc, refs = refs[0], refs[1:]
    result, q_all, k_all, low_t, high_t = refs
    nr = QROWS
    row = lax.broadcasted_iota(jnp.int32, (PAIR, PAIR), 0)
    col = lax.broadcasted_iota(jnp.int32, (PAIR, PAIR), 1)
    eye = (row == col).astype(jnp.bfloat16)
    for i, source in enumerate(q_from):
        for d in range(RING):
            slot = i * RING + d
            q_all[slot * nr : (slot + 1) * nr] = parts[source][d, 0:nr]
    low_t[HEAD_DIM:, :] = jnp.ones((VROWS - HEAD_DIM, low_t.shape[1]), jnp.bfloat16)
    high_t[HEAD_DIM:, :] = jnp.ones((VROWS - HEAD_DIM, low_t.shape[1]), jnp.bfloat16)
    at = 0
    for source, kp, vp, nk in key_from:
        part = parts[source]
        for d in range(RING):
            k_all[at + d * nk : at + (d + 1) * nk] = part[d, kp : kp + nk]
        joined = jnp.concatenate([part[d, vp : vp + nk] for d in range(RING)], axis=0)
        turned = lax.dot_general(eye, joined, NT, preferred_element_type=jnp.float32).astype(jnp.bfloat16)
        low_t[0:HEAD_DIM, at : at + RING * nk] = turned[:HEAD_DIM]
        high_t[0:HEAD_DIM, at : at + RING * nk] = turned[HEAD_DIM:]
        at += RING * nk
    values_t = (low_t, high_t)
    kept = HEAD_DIM + 8
    for block, (lowest, highest) in enumerate(groups):
        work = [(h, lowest + start, size) for start, size in cuts_of(highest - lowest, TILE) for h in range(2)]

        @pl.loop(0, BLOCK_Q // STEP_Q)
        def _(step, block=block, work=work):
            rows = pl.ds(pl.multiple_of(block * BLOCK_Q + step * STEP_Q, STEP_Q), STEP_Q)
            q = q_all[rows, :]
            lane = lax.broadcasted_iota(jnp.int32, q.shape, 1)
            zero = jnp.zeros_like(q)
            halves = (jnp.where(lane < HEAD_DIM, q, zero), jnp.where(lane < HEAD_DIM, zero, q))
            sums = [jnp.zeros((VROWS, STEP_Q), jnp.float32) for _ in range(2)]

            def score(item):
                h, start, size = item
                return lax.dot_general(
                    k_all[start : start + size, :], halves[h], NT, preferred_element_type=jnp.float32
                )

            ahead = score(work[0])
            for i, (h, start, size) in enumerate(work):
                now = ahead
                if i + 1 < len(work):
                    ahead = score(work[i + 1])
                weights = jnp.exp2(now * SCALE).astype(jnp.bfloat16)
                sums[h] = sums[h] + jnp.dot(
                    values_t[h][:, start : start + size], weights, preferred_element_type=jnp.float32
                )
            sums = [part[:kept] for part in sums]
            if block < before:
                sums = [part + acc[h, :, rows] for h, part in enumerate(sums)]
            if not last:
                for h in range(2):
                    result[h, :, rows] = sums[h]
            else:
                done = jnp.concatenate([part[:HEAD_DIM] / part[HEAD_DIM : HEAD_DIM + 1] for part in sums], axis=0)
                q_all[rows, :] = done.T.astype(jnp.bfloat16)

    if last:
        for e in range(RING):
            for d in range(RING):
                slot = e * RING + d
                along = place_ref[0] ^ d
                across = place_ref[1] ^ e
                result[along * place_ref[2] + across * place_ref[3]] = q_all[slot * nr : (slot + 1) * nr]


def attend(place, parts, q_from, key_from, groups, acc=None, last=False):
    nq = len(q_from) * RING * QROWS
    total = sum(RING * nk for _, _, _, nk in key_from)
    before = 0 if acc is None else acc.shape[2] // BLOCK_Q
    operands = list(parts) + ([] if acc is None else [acc])
    vmem = pl.BlockSpec(memory_space=pltpu.VMEM)
    if last:
        out_shape = jax.ShapeDtypeStruct((RING * RING, QROWS, PAIR), jnp.bfloat16)
    else:
        out_shape = jax.ShapeDtypeStruct((2, HEAD_DIM + 8, nq), jnp.float32)
    keys = sum(high - low for low, high in groups)
    return pl.pallas_call(
        functools.partial(attend_kernel, len(parts), q_from, key_from, groups, before, last),
        in_specs=[pl.BlockSpec(memory_space=pltpu.SMEM)] + [vmem] * len(operands),
        out_specs=vmem,
        out_shape=out_shape,
        scratch_shapes=[
            pltpu.VMEM((nq, PAIR), jnp.bfloat16),
            pltpu.VMEM((total, PAIR), jnp.bfloat16),
            pltpu.VMEM((VROWS, total), jnp.bfloat16),
            pltpu.VMEM((VROWS, total), jnp.bfloat16),
        ],
        compiler_params=pltpu.CompilerParams(vmem_limit_bytes=32 * MIB),
        cost_estimate=pl.CostEstimate(
            flops=2 * 2 * 4 * BLOCK_Q * keys * PAIR, bytes_accessed=2 * MIB, transcendentals=2 * BLOCK_Q * keys
        ),
        name="attend",
    )(place, *operands)


def project_kernel(place_ref, level_ref, got_ref, hidden_ref, w_proj_ref, w_final_ref, base_ref, slope_ref, *refs):
    velocity_ref, drift_ref, joined = refs
    for j in range(RING * RING):
        hi, lo = divmod(j, RING)
        pair = hi * place_ref[2] + lo * place_ref[3]
        joined[:, pl.ds(pl.multiple_of(pair * PAIR, PAIR), PAIR)] = got_ref[j]
    squares = jnp.zeros((QROWS, 1), jnp.float32)
    product = jnp.zeros((LAT, QROWS), jnp.float32)
    for start, size in cuts_of(D, 512):
        cols = slice(start, start + size)
        projected = jnp.dot(joined[...], w_proj_ref[:, cols], preferred_element_type=jnp.float32)
        gate = base_ref[:, cols] + level_ref[0] * slope_ref[:, cols]
        value = hidden_ref[:, cols].astype(jnp.float32) + gate * projected
        product = product + lax.dot_general(
            w_final_ref[:, cols], value.astype(jnp.bfloat16), NT, preferred_element_type=jnp.float32
        )
        squares = squares + jnp.sum(value * value, axis=1, keepdims=True)
    along = jnp.broadcast_to(squares, (QROWS, PAIR)).T[0:1]
    velocity = product * lax.rsqrt(along * (1.0 / D) + 1e-06)
    velocity_ref[...] = velocity
    drift = velocity * level_ref[1]
    drift_ref[...] = drift


def project(place, level, got, hidden, w_proj, w_final, base, slope):
    vmem = pl.BlockSpec(memory_space=pltpu.VMEM)
    smem = pl.BlockSpec(memory_space=pltpu.SMEM)
    return pl.pallas_call(
        project_kernel,
        in_specs=[smem, smem] + [vmem] * 6,
        out_specs=[vmem] * 2,
        out_shape=[
            jax.ShapeDtypeStruct((LAT, QROWS), jnp.float32),
            jax.ShapeDtypeStruct((LAT, QROWS), jnp.float32),
        ],
        scratch_shapes=[pltpu.VMEM((QROWS, HD), jnp.bfloat16)],
        compiler_params=pltpu.CompilerParams(vmem_limit_bytes=16 * MIB),
        cost_estimate=pl.CostEstimate(flops=2 * QROWS * HD * D, bytes_accessed=12 * MIB, transcendentals=0),
        name="project",
    )(place, level, got, hidden, w_proj, w_final, base, slope)


def sigma_of(index_val, total_steps):
    frac = 1.0 - index_val.astype(jnp.float32) / total_steps
    return 3.0 * frac / (1.0 + 2.0 * frac)


def per_device(
    queries, keys, values, hidden, w_proj, w_final, gate_base, gate_slope, start_latent, window_steps
):
    slots = lax.axis_size("tm")
    slot = lax.axis_index("tm")
    seat = lax.axis_index("seq")
    x, z = seat // RING, lax.rem(seat, RING)
    even = lax.rem(slot, 2) == 0
    first, second = jnp.where(even, x, z), jnp.where(even, z, x)
    place = jnp.stack([first, second, jnp.where(even, RING, 1), jnp.where(even, 1, RING), slot]).astype(jnp.int32)
    sigma_now = sigma_of(window_steps[slot], 2 * slots)
    step_size = sigma_of(window_steps[slot + 1], 2 * slots) - sigma_now
    level = jnp.stack([sigma_now, step_size])

    places, end = layout()
    starts = [0] + [kp for kp, _ in places[1:]] + [end]
    landed = first_hop(queries[0], keys[0], values[0])
    received = [second_hop(landed, start, stop) for start, stop in zip(starts, starts[1:])]
    (a0, a1), (b0, b1) = KEY_CUTS
    na, nb = a1 - a0, b1 - b0
    kb, vb = places[1][0] - starts[1], places[1][1] - starts[1]
    first_part, second_part = received
    in_a = [(e, *places[0], na) for e in range(RING)]
    acc = attend(
        place,
        [first_part[0], first_part[1], second_part[0]],
        (0, 1),
        (*in_a[:2], (2, kb, vb, nb)),
        ((0, RING * (2 * na + nb)),),
    )
    acc = attend(
        place, first_part, range(RING), in_a, ((2 * RING * na, RING * RING * na), (0, RING * RING * na)), acc
    )
    got = attend(
        place,
        [*first_part, *second_part],
        range(RING),
        [(RING + e, kb, vb, nb) for e in range(RING)],
        ((RING * nb, RING * RING * nb), (0, RING * RING * nb)),
        acc,
        True,
    )
    ahead = (lax.broadcasted_iota(jnp.int32, (SLOTS // 2, LAT, QROWS), 0) > slot // 2).astype(jnp.float32)
    from_other = jnp.broadcast_to(jnp.where(even, 0.0, 1.0), (LAT, QROWS))
    got, ahead, from_other, *operands = lax.optimization_barrier(
        (got, ahead, from_other, level, hidden[0], w_proj, w_final.T, gate_base[None], gate_slope[None])
    )
    got = lax.all_to_all(got, "seq", 0, 0, tiled=True)
    velocity, drift = project(place, operands[0], got, *operands[1:])
    other = lax.ppermute(drift, "tm", [(i, i ^ 1) for i in range(SLOTS)])
    later = (ahead * (drift + other)[None]).astype(jnp.bfloat16)
    groups = [[core + 2 * chip for chip in range(SLOTS // 2)] for core in range(2)]
    earlier = lax.all_to_all(later, "tm", 0, 0, axis_index_groups=groups, tiled=True).astype(jnp.float32)
    latents = start_latent.T + drift + from_other * other + jnp.sum(earlier, axis=0)
    return (velocity.T[None], latents.T[None])


def solution(mesh):
    placed = (
        P("tm", "seq", None),
        P("tm", "seq", None),
        P("tm", "seq", None),
        P("tm", "seq", None),
        P(),
        P(),
        P(),
        P(),
        P("seq", None),
        P(),
    )
    return jax.shard_map(
        per_device,
        mesh=mesh,
        in_specs=placed,
        out_specs=(P("tm", "seq", None), P("tm", "seq", None)),
        check_vma=False,
    )
```

profile of v0, /device:TPU:0, one launch (start us, length us, event | category | flops | bytes accessed | tf_op | source)
XLA Modules:
  0.0 115.4 jit_solution(2684107898023075105)
XLA Ops:
  0.7 4.7 %pack.1 = (bf16[4,832,128]{2,1,0:T(8,128)(2,1)}, bf16[4,832,128]{2,1,0:T(8,128)(2,1)}, bf16[4,832,128]{2,1,0:T(8,128)(2,1)}, bf16[4,832,128]{2,1,0:T(8,128)(2,1)}) custom-call(bf16[256,2048]{1,0:T(8,128)(2,1)} %bitcast.31, bf16[280,2048]{1,0:T(8,128)(2,1)} %bitcast.29, bf16[280,2048]{1,0:T(8,128)(2,1)} %bitcast.30), custom_call_target="tpu_custom_call" | custom-call | flops 872415232 | bytes 6815744 | tf_op jit(solution)/shard_map/pack/pallas_call | solution.py:114
  5.4 2.9 %collective-permute-start.2 = (bf16[4,832,128]{2,1,0:T(8,128)(2,1)}, bf16[4,832,128]{2,1,0:T(8,128)(2,1)S(1)}, u32[]{:S(2)}, u32[]{:S(2)}) collective-permute-start(bf16[4,832,128]{2,1,0:T(8,128)(2,1)} %get-tuple-element.20), channel_id=1, source_target_pairs={{0,12},{1,13},{2,14},{3,15},{4,8},{5,9},{6,10},{7,11},{8,4},{9,5},... | collective-permute-start | bytes 2555912 | tf_op jit(solution)/shard_map/ppermute | solution.py:45
  8.3 0.8 collective-permute-start.1
  9.1 0.4 collective-permute-start
  9.5 1.8 %fusion.3 = (bf16[1,384,128]{2,1,0:T(8,128)(2,1)S(1)}, bf16[1,384,128]{2,1,0:T(8,128)(2,1)}, bf16[1,384,128]{2,1,0:T(8,128)(2,1)}, bf16[1,384,128]{2,1,0:T(8,128)(2,1)}) fusion(bf16[4,832,128]{2,1,0:T(8,128)(2,1)} %get-tuple-element.17), kind=kLoop, calls=%fused_computation.16 | loop fusion | bytes 786432 | tf_op jit(solution)/shard_map/slice | solution.py:139
  11.3 0.6 fusion.11
  13.3 0.1 stack.56.place_ref
  13.4 0.1 pad_maximum_fusion.8.level_ref
  13.5 15.2 %collective-permute-done.2 = bf16[4,832,128]{2,1,0:T(8,128)(2,1)S(1)} collective-permute-done((bf16[4,832,128]{2,1,0:T(8,128)(2,1)}, bf16[4,832,128]{2,1,0:T(8,128)(2,1)S(1)}, u32[]{:S(2)}, u32[]{:S(2)}) %collective-permute-start.2) | collective-permute-done | bytes 852000 | tf_op jit(solution)/shard_map/ppermute | solution.py:45
  28.7 0.0 collective-permute-done.1
  28.8 0.8 collective-permute-done
  29.6 0.1 pad_maximum_fusion.1
  29.7 2.1 %collective-permute-start.3 = (bf16[4,448,128]{2,1,0:T(8,128)(2,1)S(1)}, bf16[4,448,128]{2,1,0:T(8,128)(2,1)S(1)}, u32[]{:S(2)}, u32[]{:S(2)}) collective-permute-start(bf16[4,448,128]{2,1,0:T(8,128)(2,1)S(1)} %pad_maximum_fusion.1), channel_id=1, source_target_pairs={{0,1},{1,0},{2,3},{3,2},{4,5},{5,4},{6,7},{7,6},{8,9},{9,8},{10,11... | collective-permute-start | bytes 1376264 | tf_op jit(solution)/shard_map/ppermute | solution.py:45
  31.8 0.1 pad_maximum_fusion.2
  31.8 3.6 %collective-permute-start.4 = (bf16[4,448,128]{2,1,0:T(8,128)(2,1)S(1)}, bf16[4,448,128]{2,1,0:T(8,128)(2,1)S(1)}, u32[]{:S(2)}, u32[]{:S(2)}) collective-permute-start(bf16[4,448,128]{2,1,0:T(8,128)(2,1)S(1)} %pad_maximum_fusion.2), channel_id=1, source_target_pairs={{0,2},{1,3},{2,0},{3,1},{4,6},{5,7},{6,4},{7,5},{8,10},{9,11},{10,... | collective-permute-start | bytes 1376264 | tf_op jit(solution)/shard_map/ppermute | solution.py:45
  35.5 0.1 pad_maximum_fusion.3
  35.6 0.1 collective-permute-start.5
  35.8 0.7 copy-done.5
  36.4 0.1 pad_maximum_fusion.5
  36.5 0.1 collective-permute-start.6
  36.6 0.0 copy-done.4
  36.6 0.1 pad_maximum_fusion.6
  36.7 4.1 %collective-permute-start.7 = (bf16[4,384,128]{2,1,0:T(8,128)(2,1)S(1)}, bf16[4,384,128]{2,1,0:T(8,128)(2,1)S(1)}, u32[]{:S(2)}, u32[]{:S(2)}) collective-permute-start(bf16[4,384,128]{2,1,0:T(8,128)(2,1)S(1)} %pad_maximum_fusion.6), channel_id=1, source_target_pairs={{0,2},{1,3},{2,0},{3,1},{4,6},{5,7},{6,4},{7,5},{8,10},{9,11},{10,... | collective-permute-start | bytes 1179656 | tf_op jit(solution)/shard_map/ppermute | solution.py:45
  40.8 0.1 pad_maximum_fusion.4.refs_2_.refs_4_
  40.8 0.1 pad_maximum_fusion.7
  40.9 0.1 pad_maximum_fusion.refs_0_
  40.9 0.0 collective-permute-done.3.refs_1_
  40.9 1.4 %collective-permute-start.8 = (bf16[4,384,128]{2,1,0:T(8,128)(2,1)S(1)}, bf16[4,384,128]{2,1,0:T(8,128)(2,1)S(1)}, u32[]{:S(2)}, u32[]{:S(2)}) collective-permute-start(bf16[4,384,128]{2,1,0:T(8,128)(2,1)S(1)} %pad_maximum_fusion.7), channel_id=1, source_target_pairs={{0,3},{1,2},{2,1},{3,0},{4,7},{5,6},{6,5},{7,4},{8,11},{9,10},{10,... | collective-permute-start | bytes 1179656 | tf_op jit(solution)/shard_map/ppermute | solution.py:45
  42.4 6.1 %attend.3.refs_4_ = f32[2,72,2048]{2,1,0:T(8,128)S(1)} custom-call(s32[5]{0:T(128)S(1)} %stack.56.place_ref, bf16[4,448,128]{2,1,0:T(8,128)(2,1)S(1)} %pad_maximum_fusion.refs_0_, bf16[4,448,128]{2,1,0:T(8,128)(2,1)S(1)} %collective-permute-done.3.refs_1_, bf16[4,384,128]{2,1,0:T(8,128)(2,1)S(1)} %pad_maximum_fusion.4.refs_2_.refs_4_), custom_call_target="tpu_custom_call" | custom-call | flops 6308233216 | bytes 2097152 | tf_op jit(solution)/shard_map/attend/pallas_call | solution.py:231
  48.5 0.0 collective-permute-done.4.refs_2_
  48.5 1.7 %collective-permute-done.5.refs_3_ = bf16[4,448,128]{2,1,0:T(8,128)(2,1)S(1)} collective-permute-done((bf16[4,448,128]{2,1,0:T(8,128)(2,1)S(1)}, bf16[4,448,128]{2,1,0:T(8,128)(2,1)S(1)}, u32[]{:S(2)}, u32[]{:S(2)}) %collective-permute-start.5) | collective-permute-done | bytes 458784 | tf_op jit(solution)/shard_map/ppermute | solution.py:45
  50.2 9.1 %attend.4.refs_8_ = f32[2,72,4096]{2,1,0:T(8,128)S(1)} custom-call(s32[5]{0:T(128)S(1)} %stack.56.place_ref, bf16[4,448,128]{2,1,0:T(8,128)(2,1)S(1)} %pad_maximum_fusion.refs_0_, bf16[4,448,128]{2,1,0:T(8,128)(2,1)S(1)} %collective-permute-done.3.refs_1_, bf16[4,448,128]{2,1,0:T(8,128)(2,1)S(1)} %collective-permute-done.4.refs_2_, ...), custom_call_target="tpu_custom_call" | custom-call | flops 9663676416 | bytes 2097152 | tf_op jit(solution)/shard_map/attend/pallas_call | solution.py:231
  59.3 0.0 slice-start.1
  59.3 0.0 slice-start.2
  59.4 0.0 collective-permute-done.6.refs_5_
  59.4 0.0 collective-permute-done.7.refs_6_
  59.4 0.0 collective-permute-done.8.refs_7_
  59.4 19.9 %attend.5 = bf16[16,256,128]{2,1,0:T(8,128)(2,1)S(1)} custom-call(s32[5]{0:T(128)S(1)} %stack.56.place_ref, bf16[4,448,128]{2,1,0:T(8,128)(2,1)S(1)} %pad_maximum_fusion.refs_0_, bf16[4,448,128]{2,1,0:T(8,128)(2,1)S(1)} %collective-permute-done.3.refs_1_, bf16[4,448,128]{2,1,0:T(8,128)(2,1)S(1)} %collective-permute-done.4.refs_2_, ...), custom_call_target="tpu_custom_call" | custom-call | flops 21609054208 | bytes 2097152 | tf_op jit(solution)/shard_map/attend/pallas_call | solution.py:231
  79.3 0.0 copy-start
  79.3 0.0 copy-start.1
  79.3 0.1 iota.7
  79.5 18.6 %all_to_all.10.got_ref = bf16[16,256,128]{2,1,0:T(8,128)(2,1)S(1)} all-to-all(bf16[16,256,128]{2,1,0:T(8,128)(2,1)S(1)} %attend.5), channel_id=1, replica_groups=mesh['tm'=8,'seq'=16] {'seq'}, dimensions={0} | all-to-all | bytes 2097152 | tf_op jit(solution)/shard_map/all_to_all | solution.py:344
  98.1 0.0 copy-start.6
  98.1 5.0 %project.1 = (f32[64,256]{1,0:T(8,128)}, f32[64,256]{1,0:T(8,128)S(1)}) custom-call(s32[5]{0:T(128)S(1)} %stack.56.place_ref, f32[2]{0:T(128)S(1)} %pad_maximum_fusion.8.level_ref, bf16[16,256,128]{2,1,0:T(8,128)(2,1)S(1)} %all_to_all.10.got_ref, bf16[256,2432]{1,0:T(8,128)(2,1)S(1)} %bitcast.27, bf16[2048,2432]{1,0:T(8,128)(2,1)S(1)} %bitcast.26, ...), custom_call_target="tpu_custom_call" | custom-call | flops 2550136832 | bytes 12582912 | tf_op jit(solution)/shard_map/project/pallas_call | solution.py:277
  103.1 0.0 collective-permute-start.9
  103.1 1.3 %collective-permute-done.9 = f32[64,256]{1,0:T(8,128)S(1)} collective-permute-done((f32[64,256]{1,0:T(8,128)S(1)}, f32[64,256]{1,0:T(8,128)S(1)}, u32[]{:S(2)}, u32[]{:S(2)}) %collective-permute-start.9) | collective-permute-done | bytes 65568 | tf_op jit(solution)/shard_map/ppermute | solution.py:346
  104.4 10.2 %all_to_all.11 = bf16[4,64,256]{2,1,0:T(8,128)(2,1)S(1)} all-to-all(bf16[4,64,256]{2,1,0:T(8,128)(2,1)S(1)} %multiply_convert_fusion), channel_id=1, replica_groups={{0,32,64,96},{16,48,80,112},{1,33,65,97},{17,49,81,113},{2,34,66,98},{1..., dimensions={0} | all-to-all | bytes 262144 | tf_op jit(solution)/shard_map/all_to_all | solution.py:349
  114.7 0.7 fusion.2
  (34 shorter events, 0.3 us)
Async XLA Ops:
  0.6 10.7 %copy-start.9 = (s32[9]{0:T(128)S(1)}, s32[9]{0:T(128)}, u32[]{:S(2)}) copy-start(s32[9]{0:T(128)} %param.19) | copy-start | bytes 112
  0.6 12.5 %copy-start.7 = (f32[2432]{0:T(1024)S(1)}, f32[2432]{0:T(1024)}, u32[]{:S(2)}) copy-start(f32[2432]{0:T(1024)} %param.16) | copy-start | bytes 29188
  0.7 12.5 %copy-start.8 = (f32[2432]{0:T(1024)S(1)}, f32[2432]{0:T(1024)}, u32[]{:S(2)}) copy-start(f32[2432]{0:T(1024)} %param.17) | copy-start | bytes 29188
  5.4 8.1 %copy-start.2 = (bf16[4,832,128]{2,1,0:T(8,128)(2,1)S(1)}, bf16[4,832,128]{2,1,0:T(8,128)(2,1)}, u32[]{:S(2)}) copy-start(bf16[4,832,128]{2,1,0:T(8,128)(2,1)} %get-tuple-element.17) | copy-start | bytes 2555908
  5.4 23.3 %collective-permute-start.2 = (bf16[4,832,128]{2,1,0:T(8,128)(2,1)}, bf16[4,832,128]{2,1,0:T(8,128)(2,1)S(1)}, u32[]{:S(2)}, u32[]{:S(2)}) collective-permute-start(bf16[4,832,128]{2,1,0:T(8,128)(2,1)} %get-tuple-element.20), channel_id=1, source_target_pairs={{0,12},{1,13},{2,14},{3,15},{4,8},{5,9},{6,10},{7,11},{8,4},{9,5},... | collective-permute-start | bytes 2555912 | tf_op jit(solution)/shard_map/ppermute | solution.py:45
  8.3 20.4 %collective-permute-start.1 = (bf16[4,832,128]{2,1,0:T(8,128)(2,1)}, bf16[4,832,128]{2,1,0:T(8,128)(2,1)S(1)}, u32[]{:S(2)}, u32[]{:S(2)}) collective-permute-start(bf16[4,832,128]{2,1,0:T(8,128)(2,1)} %get-tuple-element.19), channel_id=1, source_target_pairs={{0,8},{1,9},{2,10},{3,11},{4,12},{5,13},{6,14},{7,15},{8,0},{9,1},... | collective-permute-start | bytes 2555912 | tf_op jit(solution)/shard_map/ppermute | solution.py:45
  9.1 20.5 %collective-permute-start = (bf16[4,832,128]{2,1,0:T(8,128)(2,1)}, bf16[4,832,128]{2,1,0:T(8,128)(2,1)S(1)}, u32[]{:S(2)}, u32[]{:S(2)}) collective-permute-start(bf16[4,832,128]{2,1,0:T(8,128)(2,1)} %get-tuple-element.18), channel_id=1, source_target_pairs={{0,4},{1,5},{2,6},{3,7},{4,0},{5,1},{6,2},{7,3},{8,12},{9,13},{10,... | collective-permute-start | bytes 2555912 | tf_op jit(solution)/shard_map/ppermute | solution.py:45
  29.7 11.2 %collective-permute-start.3 = (bf16[4,448,128]{2,1,0:T(8,128)(2,1)S(1)}, bf16[4,448,128]{2,1,0:T(8,128)(2,1)S(1)}, u32[]{:S(2)}, u32[]{:S(2)}) collective-permute-start(bf16[4,448,128]{2,1,0:T(8,128)(2,1)S(1)} %pad_maximum_fusion.1), channel_id=1, source_target_pairs={{0,1},{1,0},{2,3},{3,2},{4,5},{5,4},{6,7},{7,6},{8,9},{9,8},{10,11... | collective-permute-start | bytes 1376264 | tf_op jit(solution)/shard_map/ppermute | solution.py:45
  31.8 16.7 %collective-permute-start.4 = (bf16[4,448,128]{2,1,0:T(8,128)(2,1)S(1)}, bf16[4,448,128]{2,1,0:T(8,128)(2,1)S(1)}, u32[]{:S(2)}, u32[]{:S(2)}) collective-permute-start(bf16[4,448,128]{2,1,0:T(8,128)(2,1)S(1)} %pad_maximum_fusion.2), channel_id=1, source_target_pairs={{0,2},{1,3},{2,0},{3,1},{4,6},{5,7},{6,4},{7,5},{8,10},{9,11},{10,... | collective-permute-start | bytes 1376264 | tf_op jit(solution)/shard_map/ppermute | solution.py:45
  35.5 0.9 copy-start.5
  35.6 14.7 %collective-permute-start.5 = (bf16[4,448,128]{2,1,0:T(8,128)(2,1)S(1)}, bf16[4,448,128]{2,1,0:T(8,128)(2,1)S(1)}, u32[]{:S(2)}, u32[]{:S(2)}) collective-permute-start(bf16[4,448,128]{2,1,0:T(8,128)(2,1)S(1)} %pad_maximum_fusion.3), channel_id=1, source_target_pairs={{0,3},{1,2},{2,1},{3,0},{4,7},{5,6},{6,5},{7,4},{8,11},{9,10},{10,... | collective-permute-start | bytes 1376264 | tf_op jit(solution)/shard_map/ppermute | solution.py:45
  35.7 0.9 copy-start.4
  35.7 5.0 %copy-start.3 = (bf16[1,384,128]{2,1,0:T(8,128)(2,1)S(1)}, bf16[1,384,128]{2,1,0:T(8,128)(2,1)}, u32[]{:S(2)}) copy-start(bf16[1,384,128]{2,1,0:T(8,128)(2,1)} %get-tuple-element.35) | copy-start | bytes 294916
  36.5 22.9 %collective-permute-start.6 = (bf16[4,384,128]{2,1,0:T(8,128)(2,1)S(1)}, bf16[4,384,128]{2,1,0:T(8,128)(2,1)S(1)}, u32[]{:S(2)}, u32[]{:S(2)}) collective-permute-start(bf16[4,384,128]{2,1,0:T(8,128)(2,1)S(1)} %pad_maximum_fusion.5), channel_id=1, source_target_pairs={{0,1},{1,0},{2,3},{3,2},{4,5},{5,4},{6,7},{7,6},{8,9},{9,8},{10,11... | collective-permute-start | bytes 1179656 | tf_op jit(solution)/shard_map/ppermute | solution.py:45
  36.7 22.7 %collective-permute-start.7 = (bf16[4,384,128]{2,1,0:T(8,128)(2,1)S(1)}, bf16[4,384,128]{2,1,0:T(8,128)(2,1)S(1)}, u32[]{:S(2)}, u32[]{:S(2)}) collective-permute-start(bf16[4,384,128]{2,1,0:T(8,128)(2,1)S(1)} %pad_maximum_fusion.6), channel_id=1, source_target_pairs={{0,2},{1,3},{2,0},{3,1},{4,6},{5,7},{6,4},{7,5},{8,10},{9,11},{10,... | collective-permute-start | bytes 1179656 | tf_op jit(solution)/shard_map/ppermute | solution.py:45
  40.9 18.4 %collective-permute-start.8 = (bf16[4,384,128]{2,1,0:T(8,128)(2,1)S(1)}, bf16[4,384,128]{2,1,0:T(8,128)(2,1)S(1)}, u32[]{:S(2)}, u32[]{:S(2)}) collective-permute-start(bf16[4,384,128]{2,1,0:T(8,128)(2,1)S(1)} %pad_maximum_fusion.7), channel_id=1, source_target_pairs={{0,3},{1,2},{2,1},{3,0},{4,7},{5,6},{6,5},{7,4},{8,11},{9,10},{10,... | collective-permute-start | bytes 1179656 | tf_op jit(solution)/shard_map/ppermute | solution.py:45
  50.2 47.8 %slice-start = ((s8[9961472]{0:T(1024)(128)(4,1)}), s8[4194304]{0:T(1024)(128)(4,1)S(1)}, s32[]{:S(2)}) async-start(s8[9961472]{0:T(1024)(128)(4,1)} %bitcast.25), calls=%async_computation.2 | async-start | bytes 8388608
  59.3 38.7 %slice-start.1 = ((s8[9961472]{0:T(1024)(128)(4,1)}), s8[4194304]{0:T(1024)(128)(4,1)S(1)}, s32[]{:S(2)}) async-start(s8[9961472]{0:T(1024)(128)(4,1)} %bitcast.25), calls=%async_computation.3 | async-start | bytes 8388608
  59.3 38.7 %slice-start.2 = ((s8[9961472]{0:T(1024)(128)(4,1)}), s8[1572864]{0:T(1024)(128)(4,1)S(1)}, s32[]{:S(2)}) async-start(s8[9961472]{0:T(1024)(128)(4,1)} %bitcast.25), calls=%async_computation.4 | async-start | bytes 3145728
  79.3 18.8 %copy-start = (bf16[1,256,2432]{2,1,0:T(8,128)(2,1)S(1)}, bf16[1,256,2432]{2,1,0:T(8,128)(2,1)}, u32[]{:S(2)}) copy-start(bf16[1,256,2432]{2,1,0:T(8,128)(2,1)} %param.13) | copy-start | bytes 3735556
  79.3 18.8 %copy-start.1 = (bf16[2432,64]{0,1:T(8,128)(2,1)S(1)}, bf16[2432,64]{0,1:T(8,128)(2,1)}, u32[]{:S(2)}) copy-start(bf16[2432,64]{0,1:T(8,128)(2,1)} %param.15) | copy-start | bytes 933892
  98.1 16.6 %copy-start.6 = (f32[256,64]{0,1:T(8,128)S(1)}, f32[256,64]{0,1:T(8,128)}, u32[]{:S(2)}) copy-start(f32[256,64]{0,1:T(8,128)} %param.18) | copy-start | bytes 196612
  103.1 1.3 %collective-permute-start.9 = (f32[64,256]{1,0:T(8,128)S(1)}, f32[64,256]{1,0:T(8,128)S(1)}, u32[]{:S(2)}, u32[]{:S(2)}) collective-permute-start(f32[64,256]{1,0:T(8,128)S(1)} %get-tuple-element.29), channel_id=1, source_target_pairs={{0,16},{16,0},{32,48},{48,32},{64,80},{80,64},{96,112},{112,96},{1... | collective-permute-start | bytes 196616 | tf_op jit(solution)/shard_map/ppermute | solution.py:346
where the time goes:
time: 116 us; the launch traced here: 115 us
  Pallas kernels  44.9 us (39%)
  blocking collectives  28.9 us (25%)
  waiting for transfers between devices  19 us (16%)
  starting transfers between devices  15.6 us (13%)
  local copies, waits for them, and re-layouts  3.51 us (3%)
  between operations  2.37 us (2%)
  other arithmetic  1.23 us (1%)
    pallas_call x3, Pallas kernels, attend(): pl.pallas_call(functools.partial(attend_kernel, len(parts), q_from, key_f...  35.1 us
    all_to_all x1, blocking collectives, per_device(): got = lax.all_to_all(got, 'seq', 0, 0, tiled=True)  18.6 us
    ppermute x9, waiting for transfers between devices, send(): return lax.ppermute(value, BOTH, swap_pairs(first, mask))  17.7 us
    ppermute x9, starting transfers between devices, send(): return lax.ppermute(value, BOTH, swap_pairs(first, mask))  15.6 us
    all_to_all x1, blocking collectives, per_device(): lax.all_to_all(later, 'tm', 0, 0, axis_index_groups=groups, tiled=True)  10.2 us
    pallas_call x1, Pallas kernels, project(): pl.pallas_call(project_kernel, in_specs=[smem, smem] + [vmem] * 6, out_sp...  5.01 us
    pallas_call x1, Pallas kernels, pack(): pl.pallas_call(functools.partial(pack_kernel, shifts), in_specs=[pl.Block...  4.69 us
  transfers between devices with their start and end apart: 10, of which 4 were waited for; matrix products, arithmetic and copies ran while one was open for 3% of the time, Pallas kernels for 13%

commit v1 on v0

--- a/solution.py
+++ b/solution.py
@@ -171,17 +171,18 @@
         at += RING * nk
     values_t = (low_t, high_t)
     kept = HEAD_DIM + 8
+    step_q = BLOCK_Q if last else STEP_Q
     for block, (lowest, highest) in enumerate(groups):
         work = [(h, lowest + start, size) for start, size in cuts_of(highest - lowest, TILE) for h in range(2)]
 
-        @pl.loop(0, BLOCK_Q // STEP_Q)
+        @pl.loop(0, BLOCK_Q // step_q)
         def _(step, block=block, work=work):
-            rows = pl.ds(pl.multiple_of(block * BLOCK_Q + step * STEP_Q, STEP_Q), STEP_Q)
+            rows = pl.ds(pl.multiple_of(block * BLOCK_Q + step * step_q, step_q), step_q)
             q = q_all[rows, :]
             lane = lax.broadcasted_iota(jnp.int32, q.shape, 1)
             zero = jnp.zeros_like(q)
             halves = (jnp.where(lane < HEAD_DIM, q, zero), jnp.where(lane < HEAD_DIM, zero, q))
-            sums = [jnp.zeros((VROWS, STEP_Q), jnp.float32) for _ in range(2)]
+            sums = [jnp.zeros((VROWS, step_q), jnp.float32) for _ in range(2)]
 
             def score(item):
                 h, start, size = item

time: 116 us -> 115 us (level)
  no operation moved by 1% of the time
where the time goes in v1:
time: 115 us; the launch traced here: 114 us
  Pallas kernels  43.9 us (38%)
  blocking collectives  28.8 us (25%)
  waiting for transfers between devices  19 us (17%)
  starting transfers between devices  15.6 us (14%)
  local copies, waits for them, and re-layouts  3.51 us (3%)
  between operations  2.36 us (2%)
  other arithmetic  1.23 us (1%)
    pallas_call x3, Pallas kernels, attend(): pl.pallas_call(functools.partial(attend_kernel, len(parts), q_from, key_f...  34.2 us
    all_to_all x1, blocking collectives, per_device(): got = lax.all_to_all(got, 'seq', 0, 0, tiled=True)  18.6 us
    ppermute x9, waiting for transfers between devices, send(): return lax.ppermute(value, BOTH, swap_pairs(first, mask))  17.7 us
    ppermute x9, starting transfers between devices, send(): return lax.ppermute(value, BOTH, swap_pairs(first, mask))  15.6 us
    all_to_all x1, blocking collectives, per_device(): lax.all_to_all(later, 'tm', 0, 0, axis_index_groups=groups, tiled=True)  10.2 us
    pallas_call x1, Pallas kernels, project(): pl.pallas_call(project_kernel, in_specs=[smem, smem] + [vmem] * 6, out_sp...  5.01 us
    pallas_call x1, Pallas kernels, pack(): pl.pallas_call(functools.partial(pack_kernel, shifts), in_specs=[pl.Block...  4.69 us
  transfers between devices with their start and end apart: 10, of which 4 were waited for; matrix products, arithmetic and copies ran while one was open for 3% of the time, Pallas kernels for 13%

profile of v1, /device:TPU:0, one launch (start us, length us, event | category | flops | bytes accessed | tf_op | source)
XLA Modules:
  0.0 114.4 jit_solution(991864665633177508)
XLA Ops:
  0.7 4.7 %pack.1 = (bf16[4,832,128]{2,1,0:T(8,128)(2,1)}, bf16[4,832,128]{2,1,0:T(8,128)(2,1)}, bf16[4,832,128]{2,1,0:T(8,128)(2,1)}, bf16[4,832,128]{2,1,0:T(8,128)(2,1)}) custom-call(bf16[256,2048]{1,0:T(8,128)(2,1)} %bitcast.31, bf16[280,2048]{1,0:T(8,128)(2,1)} %bitcast.29, bf16[280,2048]{1,0:T(8,128)(2,1)} %bitcast.30), custom_call_target="tpu_custom_call" | custom-call | flops 872415232 | bytes 6815744 | tf_op jit(solution)/shard_map/pack/pallas_call | solution.py:114
  5.4 2.9 %collective-permute-start.2 = (bf16[4,832,128]{2,1,0:T(8,128)(2,1)}, bf16[4,832,128]{2,1,0:T(8,128)(2,1)S(1)}, u32[]{:S(2)}, u32[]{:S(2)}) collective-permute-start(bf16[4,832,128]{2,1,0:T(8,128)(2,1)} %get-tuple-element.20), channel_id=1, source_target_pairs={{0,12},{1,13},{2,14},{3,15},{4,8},{5,9},{6,10},{7,11},{8,4},{9,5},... | collective-permute-start | bytes 2555912 | tf_op jit(solution)/shard_map/ppermute | solution.py:45
  8.3 0.8 collective-permute-start.1
  9.1 0.4 collective-permute-start
  9.5 1.8 %fusion.3 = (bf16[1,384,128]{2,1,0:T(8,128)(2,1)S(1)}, bf16[1,384,128]{2,1,0:T(8,128)(2,1)}, bf16[1,384,128]{2,1,0:T(8,128)(2,1)}, bf16[1,384,128]{2,1,0:T(8,128)(2,1)}) fusion(bf16[4,832,128]{2,1,0:T(8,128)(2,1)} %get-tuple-element.17), kind=kLoop, calls=%fused_computation.16 | loop fusion | bytes 786432 | tf_op jit(solution)/shard_map/slice | solution.py:139
  11.3 0.6 fusion.11
  13.3 0.1 stack.56.place_ref
  13.4 0.1 pad_maximum_fusion.8.level_ref
  13.5 15.2 %collective-permute-done.2 = bf16[4,832,128]{2,1,0:T(8,128)(2,1)S(1)} collective-permute-done((bf16[4,832,128]{2,1,0:T(8,128)(2,1)}, bf16[4,832,128]{2,1,0:T(8,128)(2,1)S(1)}, u32[]{:S(2)}, u32[]{:S(2)}) %collective-permute-start.2) | collective-permute-done | bytes 852000 | tf_op jit(solution)/shard_map/ppermute | solution.py:45
  28.7 0.0 collective-permute-done.1
  28.8 0.8 collective-permute-done
  29.6 0.1 pad_maximum_fusion.1
  29.7 2.1 %collective-permute-start.3 = (bf16[4,448,128]{2,1,0:T(8,128)(2,1)S(1)}, bf16[4,448,128]{2,1,0:T(8,128)(2,1)S(1)}, u32[]{:S(2)}, u32[]{:S(2)}) collective-permute-start(bf16[4,448,128]{2,1,0:T(8,128)(2,1)S(1)} %pad_maximum_fusion.1), channel_id=1, source_target_pairs={{0,1},{1,0},{2,3},{3,2},{4,5},{5,4},{6,7},{7,6},{8,9},{9,8},{10,11... | collective-permute-start | bytes 1376264 | tf_op jit(solution)/shard_map/ppermute | solution.py:45
  31.8 0.1 pad_maximum_fusion.2
  31.8 3.6 %collective-permute-start.4 = (bf16[4,448,128]{2,1,0:T(8,128)(2,1)S(1)}, bf16[4,448,128]{2,1,0:T(8,128)(2,1)S(1)}, u32[]{:S(2)}, u32[]{:S(2)}) collective-permute-start(bf16[4,448,128]{2,1,0:T(8,128)(2,1)S(1)} %pad_maximum_fusion.2), channel_id=1, source_target_pairs={{0,2},{1,3},{2,0},{3,1},{4,6},{5,7},{6,4},{7,5},{8,10},{9,11},{10,... | collective-permute-start | bytes 1376264 | tf_op jit(solution)/shard_map/ppermute | solution.py:45
  35.5 0.1 pad_maximum_fusion.3
  35.6 0.1 collective-permute-start.5
  35.8 0.7 copy-done.5
  36.4 0.1 pad_maximum_fusion.5
  36.5 0.1 collective-permute-start.6
  36.6 0.0 copy-done.4
  36.6 0.1 pad_maximum_fusion.6
  36.7 4.1 %collective-permute-start.7 = (bf16[4,384,128]{2,1,0:T(8,128)(2,1)S(1)}, bf16[4,384,128]{2,1,0:T(8,128)(2,1)S(1)}, u32[]{:S(2)}, u32[]{:S(2)}) collective-permute-start(bf16[4,384,128]{2,1,0:T(8,128)(2,1)S(1)} %pad_maximum_fusion.6), channel_id=1, source_target_pairs={{0,2},{1,3},{2,0},{3,1},{4,6},{5,7},{6,4},{7,5},{8,10},{9,11},{10,... | collective-permute-start | bytes 1179656 | tf_op jit(solution)/shard_map/ppermute | solution.py:45
  40.8 0.1 pad_maximum_fusion.4.refs_2_.refs_4_
  40.8 0.1 pad_maximum_fusion.7
  40.9 0.1 pad_maximum_fusion.refs_0_
  40.9 0.0 collective-permute-done.3.refs_1_
  40.9 1.4 %collective-permute-start.8 = (bf16[4,384,128]{2,1,0:T(8,128)(2,1)S(1)}, bf16[4,384,128]{2,1,0:T(8,128)(2,1)S(1)}, u32[]{:S(2)}, u32[]{:S(2)}) collective-permute-start(bf16[4,384,128]{2,1,0:T(8,128)(2,1)S(1)} %pad_maximum_fusion.7), channel_id=1, source_target_pairs={{0,3},{1,2},{2,1},{3,0},{4,7},{5,6},{6,5},{7,4},{8,11},{9,10},{10,... | collective-permute-start | bytes 1179656 | tf_op jit(solution)/shard_map/ppermute | solution.py:45
  42.4 6.1 %attend.3.refs_4_ = f32[2,72,2048]{2,1,0:T(8,128)S(1)} custom-call(s32[5]{0:T(128)S(1)} %stack.56.place_ref, bf16[4,448,128]{2,1,0:T(8,128)(2,1)S(1)} %pad_maximum_fusion.refs_0_, bf16[4,448,128]{2,1,0:T(8,128)(2,1)S(1)} %collective-permute-done.3.refs_1_, bf16[4,384,128]{2,1,0:T(8,128)(2,1)S(1)} %pad_maximum_fusion.4.refs_2_.refs_4_), custom_call_target="tpu_custom_call" | custom-call | flops 6308233216 | bytes 2097152 | tf_op jit(solution)/shard_map/attend/pallas_call | solution.py:232
  48.5 0.0 collective-permute-done.4.refs_2_
  48.5 1.7 %collective-permute-done.5.refs_3_ = bf16[4,448,128]{2,1,0:T(8,128)(2,1)S(1)} collective-permute-done((bf16[4,448,128]{2,1,0:T(8,128)(2,1)S(1)}, bf16[4,448,128]{2,1,0:T(8,128)(2,1)S(1)}, u32[]{:S(2)}, u32[]{:S(2)}) %collective-permute-start.5) | collective-permute-done | bytes 458784 | tf_op jit(solution)/shard_map/ppermute | solution.py:45
  50.2 9.3 %attend.4.refs_8_ = f32[2,72,4096]{2,1,0:T(8,128)S(1)} custom-call(s32[5]{0:T(128)S(1)} %stack.56.place_ref, bf16[4,448,128]{2,1,0:T(8,128)(2,1)S(1)} %pad_maximum_fusion.refs_0_, bf16[4,448,128]{2,1,0:T(8,128)(2,1)S(1)} %collective-permute-done.3.refs_1_, bf16[4,448,128]{2,1,0:T(8,128)(2,1)S(1)} %collective-permute-done.4.refs_2_, ...), custom_call_target="tpu_custom_call" | custom-call | flops 9663676416 | bytes 2097152 | tf_op jit(solution)/shard_map/attend/pallas_call | solution.py:232
  59.6 0.0 slice-start.1
  59.6 0.0 slice-start.2
  59.6 0.0 collective-permute-done.6.refs_5_
  59.6 0.0 collective-permute-done.7.refs_6_
  59.6 0.0 collective-permute-done.8.refs_7_
  59.6 18.8 %attend.5 = bf16[16,256,128]{2,1,0:T(8,128)(2,1)S(1)} custom-call(s32[5]{0:T(128)S(1)} %stack.56.place_ref, bf16[4,448,128]{2,1,0:T(8,128)(2,1)S(1)} %pad_maximum_fusion.refs_0_, bf16[4,448,128]{2,1,0:T(8,128)(2,1)S(1)} %collective-permute-done.3.refs_1_, bf16[4,448,128]{2,1,0:T(8,128)(2,1)S(1)} %collective-permute-done.4.refs_2_, ...), custom_call_target="tpu_custom_call" | custom-call | flops 21609054208 | bytes 2097152 | tf_op jit(solution)/shard_map/attend/pallas_call | solution.py:232
  78.4 0.0 copy-start
  78.4 0.0 copy-start.1
  78.4 0.1 iota.7
  78.5 18.6 %all_to_all.10.got_ref = bf16[16,256,128]{2,1,0:T(8,128)(2,1)S(1)} all-to-all(bf16[16,256,128]{2,1,0:T(8,128)(2,1)S(1)} %attend.5), channel_id=1, replica_groups=mesh['tm'=8,'seq'=16] {'seq'}, dimensions={0} | all-to-all | bytes 2097152 | tf_op jit(solution)/shard_map/all_to_all | solution.py:345
  97.2 0.0 copy-start.6
  97.2 5.0 %project.1 = (f32[64,256]{1,0:T(8,128)}, f32[64,256]{1,0:T(8,128)S(1)}) custom-call(s32[5]{0:T(128)S(1)} %stack.56.place_ref, f32[2]{0:T(128)S(1)} %pad_maximum_fusion.8.level_ref, bf16[16,256,128]{2,1,0:T(8,128)(2,1)S(1)} %all_to_all.10.got_ref, bf16[256,2432]{1,0:T(8,128)(2,1)S(1)} %bitcast.27, bf16[2048,2432]{1,0:T(8,128)(2,1)S(1)} %bitcast.26, ...), custom_call_target="tpu_custom_call" | custom-call | flops 2550136832 | bytes 12582912 | tf_op jit(solution)/shard_map/project/pallas_call | solution.py:278
  102.2 0.0 collective-permute-start.9
  102.2 1.3 %collective-permute-done.9 = f32[64,256]{1,0:T(8,128)S(1)} collective-permute-done((f32[64,256]{1,0:T(8,128)S(1)}, f32[64,256]{1,0:T(8,128)S(1)}, u32[]{:S(2)}, u32[]{:S(2)}) %collective-permute-start.9) | collective-permute-done | bytes 65568 | tf_op jit(solution)/shard_map/ppermute | solution.py:347
  103.5 10.2 %all_to_all.11 = bf16[4,64,256]{2,1,0:T(8,128)(2,1)S(1)} all-to-all(bf16[4,64,256]{2,1,0:T(8,128)(2,1)S(1)} %multiply_convert_fusion), channel_id=1, replica_groups={{0,32,64,96},{16,48,80,112},{1,33,65,97},{17,49,81,113},{2,34,66,98},{1..., dimensions={0} | all-to-all | bytes 262144 | tf_op jit(solution)/shard_map/all_to_all | solution.py:350
  113.8 0.7 fusion.2
  (34 shorter events, 0.3 us)
Async XLA Ops:
  0.6 10.7 %copy-start.9 = (s32[9]{0:T(128)S(1)}, s32[9]{0:T(128)}, u32[]{:S(2)}) copy-start(s32[9]{0:T(128)} %param.19) | copy-start | bytes 112
  0.6 12.5 %copy-start.7 = (f32[2432]{0:T(1024)S(1)}, f32[2432]{0:T(1024)}, u32[]{:S(2)}) copy-start(f32[2432]{0:T(1024)} %param.16) | copy-start | bytes 29188
  0.7 12.5 %copy-start.8 = (f32[2432]{0:T(1024)S(1)}, f32[2432]{0:T(1024)}, u32[]{:S(2)}) copy-start(f32[2432]{0:T(1024)} %param.17) | copy-start | bytes 29188
  5.4 8.1 %copy-start.2 = (bf16[4,832,128]{2,1,0:T(8,128)(2,1)S(1)}, bf16[4,832,128]{2,1,0:T(8,128)(2,1)}, u32[]{:S(2)}) copy-start(bf16[4,832,128]{2,1,0:T(8,128)(2,1)} %get-tuple-element.17) | copy-start | bytes 2555908
  5.4 23.3 %collective-permute-start.2 = (bf16[4,832,128]{2,1,0:T(8,128)(2,1)}, bf16[4,832,128]{2,1,0:T(8,128)(2,1)S(1)}, u32[]{:S(2)}, u32[]{:S(2)}) collective-permute-start(bf16[4,832,128]{2,1,0:T(8,128)(2,1)} %get-tuple-element.20), channel_id=1, source_target_pairs={{0,12},{1,13},{2,14},{3,15},{4,8},{5,9},{6,10},{7,11},{8,4},{9,5},... | collective-permute-start | bytes 2555912 | tf_op jit(solution)/shard_map/ppermute | solution.py:45
  8.3 20.4 %collective-permute-start.1 = (bf16[4,832,128]{2,1,0:T(8,128)(2,1)}, bf16[4,832,128]{2,1,0:T(8,128)(2,1)S(1)}, u32[]{:S(2)}, u32[]{:S(2)}) collective-permute-start(bf16[4,832,128]{2,1,0:T(8,128)(2,1)} %get-tuple-element.19), channel_id=1, source_target_pairs={{0,8},{1,9},{2,10},{3,11},{4,12},{5,13},{6,14},{7,15},{8,0},{9,1},... | collective-permute-start | bytes 2555912 | tf_op jit(solution)/shard_map/ppermute | solution.py:45
  9.1 20.5 %collective-permute-start = (bf16[4,832,128]{2,1,0:T(8,128)(2,1)}, bf16[4,832,128]{2,1,0:T(8,128)(2,1)S(1)}, u32[]{:S(2)}, u32[]{:S(2)}) collective-permute-start(bf16[4,832,128]{2,1,0:T(8,128)(2,1)} %get-tuple-element.18), channel_id=1, source_target_pairs={{0,4},{1,5},{2,6},{3,7},{4,0},{5,1},{6,2},{7,3},{8,12},{9,13},{10,... | collective-permute-start | bytes 2555912 | tf_op jit(solution)/shard_map/ppermute | solution.py:45
  29.7 11.2 %collective-permute-start.3 = (bf16[4,448,128]{2,1,0:T(8,128)(2,1)S(1)}, bf16[4,448,128]{2,1,0:T(8,128)(2,1)S(1)}, u32[]{:S(2)}, u32[]{:S(2)}) collective-permute-start(bf16[4,448,128]{2,1,0:T(8,128)(2,1)S(1)} %pad_maximum_fusion.1), channel_id=1, source_target_pairs={{0,1},{1,0},{2,3},{3,2},{4,5},{5,4},{6,7},{7,6},{8,9},{9,8},{10,11... | collective-permute-start | bytes 1376264 | tf_op jit(solution)/shard_map/ppermute | solution.py:45
  31.8 16.7 %collective-permute-start.4 = (bf16[4,448,128]{2,1,0:T(8,128)(2,1)S(1)}, bf16[4,448,128]{2,1,0:T(8,128)(2,1)S(1)}, u32[]{:S(2)}, u32[]{:S(2)}) collective-permute-start(bf16[4,448,128]{2,1,0:T(8,128)(2,1)S(1)} %pad_maximum_fusion.2), channel_id=1, source_target_pairs={{0,2},{1,3},{2,0},{3,1},{4,6},{5,7},{6,4},{7,5},{8,10},{9,11},{10,... | collective-permute-start | bytes 1376264 | tf_op jit(solution)/shard_map/ppermute | solution.py:45
  35.5 0.9 copy-start.5
  35.6 14.7 %collective-permute-start.5 = (bf16[4,448,128]{2,1,0:T(8,128)(2,1)S(1)}, bf16[4,448,128]{2,1,0:T(8,128)(2,1)S(1)}, u32[]{:S(2)}, u32[]{:S(2)}) collective-permute-start(bf16[4,448,128]{2,1,0:T(8,128)(2,1)S(1)} %pad_maximum_fusion.3), channel_id=1, source_target_pairs={{0,3},{1,2},{2,1},{3,0},{4,7},{5,6},{6,5},{7,4},{8,11},{9,10},{10,... | collective-permute-start | bytes 1376264 | tf_op jit(solution)/shard_map/ppermute | solution.py:45
  35.7 0.9 copy-start.4
  35.7 5.0 %copy-start.3 = (bf16[1,384,128]{2,1,0:T(8,128)(2,1)S(1)}, bf16[1,384,128]{2,1,0:T(8,128)(2,1)}, u32[]{:S(2)}) copy-start(bf16[1,384,128]{2,1,0:T(8,128)(2,1)} %get-tuple-element.35) | copy-start | bytes 294916
  36.5 23.1 %collective-permute-start.6 = (bf16[4,384,128]{2,1,0:T(8,128)(2,1)S(1)}, bf16[4,384,128]{2,1,0:T(8,128)(2,1)S(1)}, u32[]{:S(2)}, u32[]{:S(2)}) collective-permute-start(bf16[4,384,128]{2,1,0:T(8,128)(2,1)S(1)} %pad_maximum_fusion.5), channel_id=1, source_target_pairs={{0,1},{1,0},{2,3},{3,2},{4,5},{5,4},{6,7},{7,6},{8,9},{9,8},{10,11... | collective-permute-start | bytes 1179656 | tf_op jit(solution)/shard_map/ppermute | solution.py:45
  36.7 22.9 %collective-permute-start.7 = (bf16[4,384,128]{2,1,0:T(8,128)(2,1)S(1)}, bf16[4,384,128]{2,1,0:T(8,128)(2,1)S(1)}, u32[]{:S(2)}, u32[]{:S(2)}) collective-permute-start(bf16[4,384,128]{2,1,0:T(8,128)(2,1)S(1)} %pad_maximum_fusion.6), channel_id=1, source_target_pairs={{0,2},{1,3},{2,0},{3,1},{4,6},{5,7},{6,4},{7,5},{8,10},{9,11},{10,... | collective-permute-start | bytes 1179656 | tf_op jit(solution)/shard_map/ppermute | solution.py:45
  40.9 18.7 %collective-permute-start.8 = (bf16[4,384,128]{2,1,0:T(8,128)(2,1)S(1)}, bf16[4,384,128]{2,1,0:T(8,128)(2,1)S(1)}, u32[]{:S(2)}, u32[]{:S(2)}) collective-permute-start(bf16[4,384,128]{2,1,0:T(8,128)(2,1)S(1)} %pad_maximum_fusion.7), channel_id=1, source_target_pairs={{0,3},{1,2},{2,1},{3,0},{4,7},{5,6},{6,5},{7,4},{8,11},{9,10},{10,... | collective-permute-start | bytes 1179656 | tf_op jit(solution)/shard_map/ppermute | solution.py:45
  50.2 46.9 %slice-start = ((s8[9961472]{0:T(1024)(128)(4,1)}), s8[4194304]{0:T(1024)(128)(4,1)S(1)}, s32[]{:S(2)}) async-start(s8[9961472]{0:T(1024)(128)(4,1)} %bitcast.25), calls=%async_computation.2 | async-start | bytes 8388608
  59.6 37.6 %slice-start.1 = ((s8[9961472]{0:T(1024)(128)(4,1)}), s8[4194304]{0:T(1024)(128)(4,1)S(1)}, s32[]{:S(2)}) async-start(s8[9961472]{0:T(1024)(128)(4,1)} %bitcast.25), calls=%async_computation.3 | async-start | bytes 8388608
  59.6 37.6 %slice-start.2 = ((s8[9961472]{0:T(1024)(128)(4,1)}), s8[1572864]{0:T(1024)(128)(4,1)S(1)}, s32[]{:S(2)}) async-start(s8[9961472]{0:T(1024)(128)(4,1)} %bitcast.25), calls=%async_computation.4 | async-start | bytes 3145728
  78.4 18.7 %copy-start = (bf16[1,256,2432]{2,1,0:T(8,128)(2,1)S(1)}, bf16[1,256,2432]{2,1,0:T(8,128)(2,1)}, u32[]{:S(2)}) copy-start(bf16[1,256,2432]{2,1,0:T(8,128)(2,1)} %param.13) | copy-start | bytes 3735556
  78.4 18.7 %copy-start.1 = (bf16[2432,64]{0,1:T(8,128)(2,1)S(1)}, bf16[2432,64]{0,1:T(8,128)(2,1)}, u32[]{:S(2)}) copy-start(bf16[2432,64]{0,1:T(8,128)(2,1)} %param.15) | copy-start | bytes 933892
  97.2 16.6 %copy-start.6 = (f32[256,64]{0,1:T(8,128)S(1)}, f32[256,64]{0,1:T(8,128)}, u32[]{:S(2)}) copy-start(f32[256,64]{0,1:T(8,128)} %param.18) | copy-start | bytes 196612
  102.2 1.3 %collective-permute-start.9 = (f32[64,256]{1,0:T(8,128)S(1)}, f32[64,256]{1,0:T(8,128)S(1)}, u32[]{:S(2)}, u32[]{:S(2)}) collective-permute-start(f32[64,256]{1,0:T(8,128)S(1)} %get-tuple-element.29), channel_id=1, source_target_pairs={{0,16},{16,0},{32,48},{48,32},{64,80},{80,64},{96,112},{112,96},{1... | collective-permute-start | bytes 196616 | tf_op jit(solution)/shard_map/ppermute | solution.py:347
